TPU v7x, 256 devices: a whole 4x4x8 slice. The times are simulated.
256 devices in a mesh: dp: 4 (over y), expert: 8 (over x, z_hi), cuts: 8 (over z_lo, core).
Axes of the slice: x: 4, y: 4, z: 8 (z_hi: 2, z_lo: 4; z = z_hi * 4 + z_lo), core: 2. Of those that a mesh axis runs over, the one named last changes fastest.
Arguments:
- tokens: bfloat16 [4096, 3072], P(('dp', 'expert'), 'cuts'), may hold values from -6 to 6
- cotangent: bfloat16 [4096, 3072], P(('dp', 'expert'), 'cuts'), may hold values from -6 to 6
- combine: float32 [4096, 2], P(('dp', 'expert')), may hold values from 0.25 to 1
- expert_ids: int32 [4096, 2], P(('dp', 'expert')), may hold values from 0 to 7, as said below
- slot_ids: int32 [4096, 2], P(('dp', 'expert')), may hold values from 0 to 35, as said below
- keep_mask: int32 [4096, 2], P(('dp', 'expert')), may hold values from 0 to 1, as said below
- w_gate: bfloat16 [8, 3072, 8192], P('expert', None, ('dp', 'cuts')), may hold values from -0.109375 to 0.109375
- w_up: bfloat16 [8, 3072, 8192], P('expert', None, ('dp', 'cuts')), may hold values from -0.109375 to 0.109375
- w_down: bfloat16 [8, 8192, 3072], P('expert', ('dp', 'cuts')), may hold values from -0.0625 to 0.0625
Outputs:
- token_grad: bfloat16 [4096, 3072], P(('dp', 'expert'), 'cuts')
- grad_gate: bfloat16 [8, 3072, 8192], P('expert', None, ('dp', 'cuts'))
- grad_up: bfloat16 [8, 3072, 8192], P('expert', None, ('dp', 'cuts'))
- grad_down: bfloat16 [8, 8192, 3072], P('expert', ('dp', 'cuts'))
Inputs may be any that keep to these rules, and one draw needn't show every extreme that they name: `expert_ids`: each token names 2 different experts. `slot_ids`: within the 128 rows of one block, the choices are given slots in order of choice (all first choices before second ones) and then of row, counted for each expert; a choice whose count reaches 36 is dropped and has slot 0. In the rows of every index of dp, one expert is filled to 36 from every block. `keep_mask`: 1 exactly where the choice's count in its block is under 36.
All inputs are finite; a program needn't handle non-finite values.
Results may differ from a plain program's by a relative error of at most 0.0058.
Values may be sent and summed in bfloat16 or wider, within the bound.
No kernel may reach another device: no remote copies, remote signals or barrier semaphores. Data moves between devices by JAX's collectives and lax.ppermute only.
A program may use at most 128 MiB of HBM per device.

v0:
```python
import jax
import jax.numpy as jnp
from jax import lax
from jax.sharding import PartitionSpec as P


def shards(tokens, cotangent, combine, expert_ids, slot_ids, keep_mask, w_gate, w_up, w_down):
    experts = lax.axis_size("expert")
    data_count = lax.axis_size("dp")
    cut_count = lax.axis_size("cuts")
    tok_rows, feature_cut = tokens.shape
    top_count = expert_ids.shape[1]
    model_width = w_gate.shape[1]
    capacity = 9 * tok_rows * top_count // (8 * experts)
    slots_all = experts * capacity
    target = expert_ids * capacity + slot_ids
    kept = keep_mask > 0
    positions = jnp.arange(slots_all, dtype=jnp.int32)[:, None]
    widened = cotangent.astype(jnp.float32)
    routes = [
        (positions == target[:, index][None, :]) & kept[:, index][None, :]
        for index in range(top_count)
    ]
    either = routes[0]
    index = 1
    either = either | routes[index]
    sent_tokens = jnp.dot(
        either.astype(jnp.bfloat16), tokens, preferred_element_type=jnp.float32
    ).astype(jnp.bfloat16)
    sent_scaled = jnp.zeros((slots_all, feature_cut), jnp.float32)
    for index in range(top_count):
        scaled = (combine[:, index : index + 1] * widened).astype(jnp.bfloat16)
        sent_scaled = sent_scaled + jnp.dot(
            routes[index].astype(jnp.bfloat16), scaled, preferred_element_type=jnp.float32
        )
    sent_scaled = sent_scaled.astype(jnp.bfloat16)
    received_tokens, received_scaled = (
        lax.all_to_all(
            sent_tokens.reshape(experts, capacity, feature_cut),
            "expert",
            split_axis=0,
            concat_axis=0,
            tiled=True,
        ),
        lax.all_to_all(
            sent_scaled.reshape(experts, capacity, feature_cut),
            "expert",
            split_axis=0,
            concat_axis=0,
            tiled=True,
        ),
    )
    collected_token_rows, collected_scaled_rows = (
        lax.all_gather(
            received_tokens.reshape(1, slots_all, feature_cut), ("dp", "cuts"), axis=0, tiled=True
        ),
        lax.all_gather(
            received_scaled.reshape(1, slots_all, feature_cut), ("dp", "cuts"), axis=0, tiled=True
        ),
    )
    collected_token_rows = collected_token_rows.reshape(
        data_count, cut_count, slots_all, feature_cut
    )
    collected_scaled_rows = collected_scaled_rows.reshape(
        data_count, cut_count, slots_all, feature_cut
    )
    gate_weight_block = w_gate[0].reshape(cut_count, feature_cut, -1)
    up_weight_block = w_up[0].reshape(cut_count, feature_cut, -1)
    down_weight_block = w_down[0].reshape(-1, cut_count, feature_cut)
    gate_pre = jnp.einsum(
        "mvla,vaw->mlw", collected_token_rows, gate_weight_block, preferred_element_type=jnp.float32
    )
    up_pre = jnp.einsum(
        "mvla,vaw->mlw", collected_token_rows, up_weight_block, preferred_element_type=jnp.float32
    )
    squash = jax.nn.sigmoid(gate_pre)
    active = gate_pre * squash
    hidden_state = (active * up_pre).astype(jnp.bfloat16)
    hidden_grad = jnp.einsum(
        "tnpl,onl->tpo",
        collected_scaled_rows,
        down_weight_block,
        preferred_element_type=jnp.float32,
    )
    gate_gradient = (hidden_grad * up_pre * (squash * (1.0 + gate_pre * (1.0 - squash)))).astype(
        jnp.bfloat16
    )
    up_gradient = (hidden_grad * active).astype(jnp.bfloat16)
    grad_gate = (
        jnp.einsum(
            "hiyb,hys->ibs", collected_token_rows, gate_gradient, preferred_element_type=jnp.float32
        )
        .astype(jnp.bfloat16)
        .reshape(1, model_width, -1)
    )
    grad_up = (
        jnp.einsum(
            "hiyb,hys->ibs", collected_token_rows, up_gradient, preferred_element_type=jnp.float32
        )
        .astype(jnp.bfloat16)
        .reshape(1, model_width, -1)
    )
    grad_down = (
        jnp.einsum(
            "hpt,hmpu->tmu", hidden_state, collected_scaled_rows, preferred_element_type=jnp.float32
        )
        .astype(jnp.bfloat16)
        .reshape(1, -1, model_width)
    )
    partial_terms = jnp.einsum(
        "ynh,jqh->yjnq", gate_gradient, gate_weight_block, preferred_element_type=jnp.float32
    ) + jnp.einsum(
        "ynh,jqh->yjnq", up_gradient, up_weight_block, preferred_element_type=jnp.float32
    )
    partial_terms = partial_terms.reshape(data_count * cut_count, slots_all, feature_cut)
    own_rows = lax.psum_scatter(partial_terms, ("dp", "cuts"), scatter_dimension=0, tiled=True)[0]
    returned = lax.all_to_all(
        own_rows.reshape(experts, capacity, feature_cut),
        "expert",
        split_axis=0,
        concat_axis=0,
        tiled=True,
    ).reshape(slots_all, feature_cut)
    token_grad = jnp.zeros((tok_rows, feature_cut), jnp.float32)
    for index in range(top_count):
        picked = jnp.take(returned, target[:, index], axis=0)
        token_grad = token_grad + jnp.where(kept[:, index : index + 1], picked, 0.0)
    return (token_grad.astype(jnp.bfloat16), grad_gate, grad_up, grad_down)


def solution(mesh):
    return jax.shard_map(
        shards,
        mesh=mesh,
        in_specs=(
            P(("dp", "expert"), "cuts"),
            P(("dp", "expert"), "cuts"),
            P(("dp", "expert"), None),
            P(("dp", "expert"), None),
            P(("dp", "expert"), None),
            P(("dp", "expert"), None),
            P("expert", None, ("dp", "cuts")),
            P("expert", None, ("dp", "cuts")),
            P("expert", ("dp", "cuts"), None),
        ),
        out_specs=(
            P(("dp", "expert"), "cuts"),
            P("expert", None, ("dp", "cuts")),
            P("expert", None, ("dp", "cuts")),
            P("expert", ("dp", "cuts"), None),
        ),
        check_vma=False,
    )
```

profile of v0, /device:TPU:2, one launch (start us, length us, event | category | flops | bytes accessed | tf_op | source)
XLA Modules:
  0.0 395.9 jit_solution(3697070514261589913)
XLA Ops:
  7.2 0.0 copy-start
  7.2 0.0 copy-start.9
  7.2 0.0 copy-start.8
  7.2 0.0 all-gather.5.cloned.1.call-start
  7.2 0.8 broadcast_compare_fusion
  8.1 0.7 multiply_add_fusion
  8.8 1.1 convolution_convert_fusion
  9.9 21.3 %all_to_all.15 = bf16[8,36,384]{2,1,0:T(8,128)(2,1)S(1)} all-to-all(bf16[8,36,384]{2,1,0:T(8,128)(2,1)S(1)} %reshape.53), channel_id=1, replica_groups=mesh['dp'=4,'expert'=8,'cuts'=8] {'expert'}, dimensions={0} | all-to-all | bytes 442368 | tf_op jit(solution)/shard_map/all_to_all | solution.py:38
  31.2 0.7 reshape.54
  32.0 0.0 copy-start.1
  32.0 0.0 all-gather.5.cloned.1.call-update
  32.0 0.0 all-gather.3.cloned.1.call-start
  32.0 0.0 copy-done.9
  32.1 0.0 copy-done.8
  32.1 0.3 fusion.21
  32.4 1.0 fusion.6
  33.3 1.0 reshape.50
  34.3 15.3 %all_to_all.16 = bf16[8,36,384]{2,1,0:T(8,128)(2,1)} all-to-all(bf16[8,36,384]{2,1,0:T(8,128)(2,1)S(1)} %reshape.50), channel_id=1, replica_groups=mesh['dp'=4,'expert'=8,'cuts'=8] {'expert'}, dimensions={0} | all-to-all | bytes 442368 | tf_op jit(solution)/shard_map/all_to_all | solution.py:45
  49.6 1.7 reshape.51
  51.3 0.0 all-gather.3.cloned.1.call-update
  51.3 0.0 reduce-scatter.2.cloned.1.call-start
  51.4 0.0 copy-done.1
  51.4 1.4 copy.33
  52.8 46.3 %all-gather.5.cloned.1.call-done = bf16[32,288,384]{2,1,0:T(8,128)(2,1)} async-done(((bf16[1,288,384]{2,1,0:T(8,128)(2,1)}), bf16[32,288,384]{2,1,0:T(8,128)(2,1)}) %all-gather.5.cloned.1.call-update) | async-done | bytes 7077904 | tf_op jit(solution)/shard_map/all_gather | solution.py:54
  99.1 0.0 copy-done
  99.1 0.0 copy-start.3
  99.1 0.0 copy-start.10
  99.1 6.2 %convolution_bitcast_fusion = f32[4,288,256]{2,1,0:T(8,128)} fusion(bf16[4,8,288,384]{3,2,1,0:T(8,128)(2,1)} %bitcast.99, bf16[8,384,256,1]{2,1,0,3:T(8,128)(2,1)S(1)} %bitcast.91), kind=kOutput, calls=%fused_computation.10 | convolution fusion | flops 1811939328 | bytes 9830400 | tf_op jit(solution)/shard_map/mvla,vaw->mlw/dot_general | solution.py:70
  105.3 0.0 copy-done.3
  105.3 0.0 copy-done.10
  105.3 0.0 copy-start.2
  105.3 3.0 convolution_bitcast_fusion.1
  108.3 59.7 %all-gather.3.cloned.1.call-done = bf16[32,288,384]{2,1,0:T(8,128)(2,1)} async-done(((bf16[1,288,384]{2,1,0:T(8,128)(2,1)}), bf16[32,288,384]{2,1,0:T(8,128)(2,1)}) %all-gather.3.cloned.1.call-update) | async-done | bytes 7077904 | tf_op jit(solution)/shard_map/all_gather | solution.py:57
  168.0 0.0 copy-done.2
  168.0 5.9 %fusion.8 = (bf16[4,288,256,1]{2,1,3,0:T(8,128)(2,1)S(1)}, bf16[4,288,256]{2,1,0:T(8,128)(2,1)S(1)}) fusion(f32[4,288,256]{2,1,0:T(8,128)} %convolution_bitcast_fusion, f32[4,288,256]{2,1,0:T(8,128)} %convolution_bitcast_fusion.1, bf16[4,8,288,384]{3,2,1,0:T(8,128)(2,1)} %bitcast.103, bf16[256,8,384]{2,1,0:T(8,128)(2,1)S(1)} %bitcast.96), kind=kOutput, calls=%fused_computation.20 | convolution fusion | flops 1815773184 | bytes 12189696 | tf_op jit(solution)/shard_map/tnpl,onl->tpo/dot_general | solution.py:79
  173.9 0.0 copy-start.5
  173.9 0.0 copy-start.6
  173.9 0.0 copy-start.4
  173.9 2.0 fusion.12
  176.0 0.0 copy-done.5
  176.0 0.0 copy-done.6
  176.0 0.0 copy-done.4
  176.0 6.1 %convolution_add_fusion = f32[4,288,8,384]{3,1,2,0:T(8,128)} fusion(f32[4,288,8,384]{3,1,2,0:T(8,128)S(1)} %fusion.12, bf16[4,288,256,1]{2,1,3,0:T(8,128)(2,1)S(1)} %get-tuple-element.17, bf16[8,384,256,1]{2,1,0,3:T(8,128)(2,1)S(1)} %bitcast.98), kind=kOutput, calls=%fused_computation.2 | convolution fusion | flops 1815478272 | bytes 30474240 | tf_op jit(solution)/shard_map/ynh,jqh->yjnq/dot_general | solution.py:112
  182.1 0.0 copy-start.11
  182.1 0.0 reduce-scatter.2.cloned.1.call-update
  182.2 1.2 copy-done.11
  183.4 6.8 %bitcast_convert_fusion = bf16[256,8,384]{2,0,1:T(8,128)(2,1)} fusion(bf16[4,8,288,384]{3,2,1,0:T(8,128)(2,1)} %bitcast.104, f32[4,288,256]{2,1,0:T(8,128)} %convolution_bitcast_fusion.1, f32[4,288,256]{2,1,0:T(8,128)S(1)} %copy-done.11), kind=kOutput, calls=%fused_computation.3 | convolution fusion | flops 1814495232 | bytes 11010048 | tf_op jit(solution)/shard_map/hpt,hmpu->tmu/dot_general | solution.py:104
  190.2 0.0 copy-start.7
  190.2 169.7 %reduce-scatter.2.cloned.1.call-done = f32[1,288,384]{2,1,0:T(8,128)} async-done(((f32[32,288,384]{2,1,0:T(8,128)}), f32[1,288,384]{2,1,0:T(8,128)}) %reduce-scatter.2.cloned.1.call-update) | async-done | bytes 442384 | tf_op jit(solution)/shard_map/reduce_scatter | solution.py:116
  359.9 1.8 reshape_squeeze.15
  361.7 7.9 %all-to-all-start.2 = ((f32[8,36,384]{2,1,0:T(8,128)}), f32[8,36,384]{2,1,0:T(8,128)}, u32[]{:S(2)}, u32[]{:S(2)}) async-start(f32[8,36,384]{2,1,0:T(8,128)} %reshape_squeeze.15), calls=%async_computation.3 | async-start | bytes 983040 | tf_op jit(solution)/shard_map/all_to_all | solution.py:117
  369.6 0.0 copy-done.7
  369.6 6.4 %bitcast_convert_fusion.1 = bf16[8,384,256]{2,1,0:T(8,128)(2,1)} fusion(bf16[4,8,288,384]{3,2,1,0:T(8,128)(2,1)} %bitcast.100, bf16[4,288,256,1]{2,1,3,0:T(8,128)(2,1)S(1)} %copy-done.7), kind=kOutput, calls=%fused_computation.4 | convolution fusion | flops 1812725760 | bytes 9240576 | tf_op jit(solution)/shard_map/hiyb,hys->ibs/dot_general | solution.py:97
  376.0 1.7 copy.25
  377.8 1.7 copy.26
  379.5 6.5 %bitcast_convert_fusion.2 = bf16[8,384,256]{2,1,0:T(8,128)(2,1)} fusion(bf16[4,8,288,384]{3,2,1,0:T(8,128)(2,1)} %bitcast.101, bf16[4,288,256]{2,1,0:T(8,128)(2,1)} %copy-done.5), kind=kOutput, calls=%fused_computation.5 | convolution fusion | flops 1812725760 | bytes 9240576 | tf_op jit(solution)/shard_map/hiyb,hys->ibs/dot_general | solution.py:90
  386.0 0.0 all-to-all-done.2
  386.0 1.1 reshape.57
  387.1 0.8 gather_fusion.1
  387.8 0.8 gather_fusion
  388.6 0.8 fusion.18
  (6 shorter events, 0.1 us)
Async XLA Ops:
  7.2 91.9 %copy-start = (bf16[1,3072,256]{2,1,0:T(8,128)(2,1)S(1)}, bf16[1,3072,256]{2,1,0:T(8,128)(2,1)}, u32[]{:S(2)}) copy-start(bf16[1,3072,256]{2,1,0:T(8,128)(2,1)} %param.17) | copy-start | bytes 4718596
  7.2 24.9 %copy-start.9 = (f32[128,2]{0,1:T(2,128)S(1)}, f32[128,2]{0,1:T(2,128)}, u32[]{:S(2)}) copy-start(f32[128,2]{0,1:T(2,128)} %param.13) | copy-start | bytes 3076
  7.2 24.9 %copy-start.8 = (bf16[128,384]{1,0:T(8,128)(2,1)S(1)}, bf16[128,384]{1,0:T(8,128)(2,1)}, u32[]{:S(2)}) copy-start(bf16[128,384]{1,0:T(8,128)(2,1)} %param.12) | copy-start | bytes 294916
  7.2 91.9 %all-gather.5.cloned.1.call-start = ((), (), s32[]{:S(2)}) async-start(), calls=%async_computation.5 | async-start | bytes 7299072 | tf_op jit(solution)/shard_map/all_gather | solution.py:54
  32.0 19.4 %copy-start.1 = (bf16[1,256,3072]{2,1,0:T(8,128)(2,1)S(1)}, bf16[1,256,3072]{2,1,0:T(8,128)(2,1)}, u32[]{:S(2)}) copy-start(bf16[1,256,3072]{2,1,0:T(8,128)(2,1)} %param.19) | copy-start | bytes 4718596
  32.0 136.0 %all-gather.3.cloned.1.call-start = ((), (), s32[]{:S(2)}) async-start(), calls=%async_computation.4 | async-start | bytes 7299072 | tf_op jit(solution)/shard_map/all_gather | solution.py:57
  51.3 308.6 %reduce-scatter.2.cloned.1.call-start = ((), (), s32[]{:S(2)}) async-start(), calls=%async_computation.6 | async-start | bytes 14598144 | tf_op jit(solution)/shard_map/reduce_scatter | solution.py:116
  99.1 6.2 %copy-start.3 = (bf16[1,3072,256]{2,1,0:T(8,128)(2,1)S(1)}, bf16[1,3072,256]{2,1,0:T(8,128)(2,1)}, u32[]{:S(2)}) copy-start(bf16[1,3072,256]{2,1,0:T(8,128)(2,1)} %param.18) | copy-start | bytes 4718596
  99.1 6.2 %copy-start.10 = (bf16[32,288,384]{2,1,0:T(8,128)(2,1)S(1)}, bf16[32,288,384]{2,1,0:T(8,128)(2,1)}, u32[]{:S(2)}) copy-start(bf16[32,288,384]{2,1,0:T(8,128)(2,1)} %all-gather.5.cloned.1.call-done) | copy-start | bytes 21233668
  105.3 62.7 %copy-start.2 = (bf16[32,8,8,384]{3,2,1,0:T(8,128)(2,1)S(1)}, bf16[32,8,8,384]{3,2,1,0:T(8,128)(2,1)}, u32[]{:S(2)}) copy-start(bf16[32,8,8,384]{3,2,1,0:T(8,128)(2,1)} %copy.33) | copy-start | bytes 4718596
  173.9 2.1 copy-start.5
  173.9 2.1 copy-start.6
  173.9 2.1 copy-start.4
  182.1 1.3 copy-start.11
  190.2 179.4 %copy-start.7 = (bf16[4,288,256,1]{2,1,3,0:T(8,128)(2,1)S(1)}, bf16[4,288,256,1]{2,1,3,0:T(8,128)(2,1)}, u32[]{:S(2)}) copy-start(bf16[4,288,256,1]{2,1,3,0:T(8,128)(2,1)} %copy-done.6) | copy-start | bytes 1769476
  361.7 24.3 %all-to-all-start.2 = ((f32[8,36,384]{2,1,0:T(8,128)}), f32[8,36,384]{2,1,0:T(8,128)}, u32[]{:S(2)}, u32[]{:S(2)}) async-start(f32[8,36,384]{2,1,0:T(8,128)} %reshape_squeeze.15), calls=%async_computation.3 | async-start | bytes 983040 | tf_op jit(solution)/shard_map/all_to_all | solution.py:117
Sparse Core Ops, SparseCore 0:
  32.1 66.9 all-gather.4
  100.9 66.9 all-gather.2
  182.3 177.5 reduce-scatter.1
where the time goes:
time: 396 us
  waiting for transfers between devices  276 us (70%)
  matrix products  45.3 us (11%)
  blocking collectives  36.6 us (9%)
  local copies, waits for them, and re-layouts  14 us (4%)
  between operations  13.9 us (4%)
  starting transfers between devices  8.05 us (2%)
    reduce_scatter x1, waiting for transfers between devices, shards(): lax.psum_scatter(partial_terms, ('dp', 'cuts'), scatter_dimension=0, tile...  170 us
    all_gather x1, waiting for transfers between devices, shards(): lax.all_gather(received_scaled.reshape(1, slots_all, feature_cut), ('dp',...  59.7 us
    all_gather x1, waiting for transfers between devices, shards(): lax.all_gather(received_tokens.reshape(1, slots_all, feature_cut), ('dp',...  46.3 us
    all_to_all x1, blocking collectives, shards(): lax.all_to_all(sent_tokens.reshape(experts, capacity, feature_cut), 'expe...  21.3 us
    all_to_all x1, blocking collectives, shards(): lax.all_to_all(sent_scaled.reshape(experts, capacity, feature_cut), 'expe...  15.3 us
    all_to_all x1, starting transfers between devices, shards(): lax.all_to_all(own_rows.reshape(experts, capacity, feature_cut), 'expert'...  7.93 us
  transfers between devices with their start and end apart: 4, of which 3 were waited for; matrix products, arithmetic and copies ran while one was open for 10% of the time, Pallas kernels for 0%

commit v1 on v0

v1 whole, which is shorter than its diff:
```python
import jax
import jax.numpy as jnp
from jax import lax
from jax.experimental import pallas as pl
from jax.experimental.pallas import tpu as pltpu
from jax.sharding import Mesh, PartitionSpec as P

TOPK = 2
BF = jnp.bfloat16
F32 = jnp.float32


def shift(size, step):
    return [(i, (i + step) % size) for i in range(size)]


def zshift(flip, step):
    return [(h * 4 + l, (h ^ flip) * 4 + (l + step) % 4) for h in range(2) for l in range(4)]


def up_kernel(rows_ref, gate_ref, up_ref, down_ref, grads_ref, hidden_ref):
    cuts, _, width = rows_ref.shape[1:]
    cut = width // 2
    gate = up = back = None
    for v in range(cuts):
        part = pl.ds(v * cut, cut)
        token_rows = rows_ref[0, v, :, :cut]
        scaled_rows = rows_ref[0, v, :, cut:]
        g = jnp.dot(token_rows, gate_ref[part, :], preferred_element_type=F32)
        u = jnp.dot(token_rows, up_ref[part, :], preferred_element_type=F32)
        h = lax.dot_general(
            scaled_rows,
            down_ref[:, part],
            (((1,), (1,)), ((), ())),
            preferred_element_type=F32,
        )
        gate = g if gate is None else gate + g
        up = u if up is None else up + u
        back = h if back is None else back + h
    squash = jax.nn.sigmoid(gate)
    active = gate * squash
    units = gate.shape[1]
    hidden_ref[0] = (active * up).astype(BF)
    grads_ref[0, :, :units] = (back * up * (squash * (1.0 + gate * (1.0 - squash)))).astype(BF)
    grads_ref[0, :, units:] = (back * active).astype(BF)


def up_pass(collected, gate_w, up_w, down_w):
    blocks, cuts, rows, width = collected.shape
    model, units = gate_w.shape
    return pl.pallas_call(
        up_kernel,
        grid=(blocks,),
        in_specs=[
            pl.BlockSpec((1, cuts, rows, width), lambda i: (i, 0, 0, 0)),
            pl.BlockSpec((model, units), lambda i: (0, 0)),
            pl.BlockSpec((model, units), lambda i: (0, 0)),
            pl.BlockSpec((units, model), lambda i: (0, 0)),
        ],
        out_specs=[
            pl.BlockSpec((1, rows, 2 * units), lambda i: (i, 0, 0)),
            pl.BlockSpec((1, rows, units), lambda i: (i, 0, 0)),
        ],
        out_shape=[
            jax.ShapeDtypeStruct((blocks, rows, 2 * units), BF),
            jax.ShapeDtypeStruct((blocks, rows, units), BF),
        ],
        compiler_params=pltpu.CompilerParams(vmem_limit_bytes=48 * 1024 * 1024),
        cost_estimate=pl.CostEstimate(
            flops=6 * blocks * rows * model * units,
            bytes_accessed=2 * blocks * rows * 2 * model,
            transcendentals=blocks * rows * units,
        ),
    )(collected, gate_w, up_w, down_w)


def shards(tokens, cotangent, combine, expert_ids, slot_ids, keep_mask, w_gate, w_up, w_down):
    experts = 8
    tok_rows, cut = tokens.shape
    capacity = 9 * tok_rows * TOPK // (8 * experts)
    slots = experts * capacity
    zh, zl = lax.axis_index("zh"), lax.axis_index("zl")
    y, c = lax.axis_index("y"), lax.axis_index("c")
    kept = keep_mask > 0

    place = jnp.where(kept, (expert_ids // 2) * (2 * capacity) + slot_ids, -1)
    mine = jnp.where((expert_ids % 2) == zh, place, -1)
    theirs = jnp.where((expert_ids % 2) != zh, place, -1)
    theirs = lax.ppermute(theirs, "zh", [(0, 1), (1, 0)])

    target = jnp.where(kept, expert_ids * capacity + slot_ids, -1)
    positions = jnp.arange(slots, dtype=jnp.int32)[:, None]
    routes = [positions == target[:, k][None, :] for k in range(TOPK)]
    pick = (routes[0] | routes[1]).astype(BF)
    weight = sum(
        jnp.sum(jnp.where(routes[k], combine[:, k][None, :], 0.0), axis=1, keepdims=True)
        for k in range(TOPK)
    )
    both = jnp.dot(pick, jnp.concatenate([tokens, cotangent], axis=1), preferred_element_type=F32)
    sent = jnp.concatenate(
        [both[:, :cut].astype(BF), (both[:, cut:] * weight).astype(BF)], axis=1
    )
    received = lax.all_to_all(
        sent.reshape(experts, capacity, 2 * cut), ("x", "zh"), split_axis=0, concat_axis=0, tiled=True
    )
    collected = lax.all_gather(
        received.reshape(1, slots, 2 * cut), ("y", "zl", "c"), axis=0, tiled=True
    ).reshape(4, 8, slots, 2 * cut)

    gate_w, up_w, down_w = w_gate[0], w_up[0], w_down[0]
    grads, hidden = up_pass(collected, gate_w, up_w, down_w)
    units = gate_w.shape[1]

    def turned(owner):
        joined = jnp.concatenate([gate_w, up_w], axis=1).reshape(4, 2, cut, 2 * units)
        joined = jnp.concatenate([joined, joined[:3]], axis=0)
        return lax.dynamic_slice(joined, (zl, owner, 0, 0), (4, 1, cut, 2 * units)).reshape(
            4 * cut, 2 * units
        )

    near, far = turned(c), turned(1 - c)
    half = 2 * cut
    swap = [(0, 1), (1, 0)]

    def block(step):
        return lax.dynamic_index_in_dim(grads, (y + step) % 4, 0, keepdims=False)

    def product(rows, weights):
        return lax.dot_general(rows, weights, (((1,), (1,)), ((), ())), preferred_element_type=F32)

    def halves(step):
        rows = block(step)
        got = lax.ppermute(product(rows, far).astype(BF), "c", swap).astype(F32)
        return (
            product(rows, near[:half]) + got[:, :half],
            product(rows, near[half:]) + got[:, half:],
        )

    up_y = lambda v: lax.ppermute(v.astype(BF), "y", shift(4, 1)).astype(F32)
    down_y = lambda v: lax.ppermute(v.astype(BF), "y", shift(4, -1)).astype(F32)
    across = halves(2)
    relay_a = up_y(across[0])
    relay_b = down_y(across[1])
    above, below = halves(1), halves(3)
    from_below_b = up_y(above[1])
    from_above_a = down_y(below[0])
    from_below_a = up_y(above[0] + relay_a)
    from_above_b = down_y(below[1] + relay_b)
    own = halves(0)
    rows = jnp.concatenate(
        [own[0] + from_below_a + from_above_a, own[1] + from_below_b + from_above_b], axis=1
    ).astype(BF)

    x = lax.axis_index("x")
    rows = rows.reshape(4, 2 * capacity, 4 * cut)
    returned = [lax.dynamic_index_in_dim(rows, x, 0, keepdims=False)]
    for step in (1, 3, 2):
        piece = lax.dynamic_index_in_dim(rows, (x + step) % 4, 0, keepdims=False)
        returned.append(lax.ppermute(piece, "x", shift(4, step)))
    returned = jnp.concatenate([returned[0], returned[1], returned[3], returned[2]], axis=0)

    slot_base = jnp.arange(slots, dtype=jnp.int32)[None, :]
    def spread(places, owner_zh):
        owner = places // (2 * capacity)
        slot = places % (2 * capacity)
        column = ((x - owner) % 4) * (2 * capacity) + owner_zh * capacity + slot
        column = jnp.where(places >= 0, column, -1)
        return ((slot_base == column[:, 0:1]) | (slot_base == column[:, 1:2])).astype(BF)

    routes_back = jnp.concatenate([spread(mine, zh), spread(theirs, 1 - zh)], axis=0)
    parts = jnp.dot(routes_back, returned, preferred_element_type=F32).astype(BF)
    parts = parts.reshape(2, tok_rows, 4, cut)
    total = parts[0, :, 0].astype(F32)
    for flip in range(2):
        for step in range(4):
            if flip == 0 and step == 0:
                continue
            got = lax.ppermute(parts[flip, :, step], ("zh", "zl"), zshift(flip, step))
            total = total + got.astype(F32)
    token_grad = total.astype(BF)

    grads_all = grads.reshape(4, slots, 2 * units)
    token_part = collected[..., :cut]
    scaled_part = collected[..., cut:]
    grad_gate = jnp.einsum(
        "hiyb,hys->ibs", token_part, grads_all[..., :units], preferred_element_type=F32
    )
    grad_up = jnp.einsum(
        "hiyb,hys->ibs", token_part, grads_all[..., units:], preferred_element_type=F32
    )
    grad_down = jnp.einsum("hpt,hmpu->tmu", hidden, scaled_part, preferred_element_type=F32)
    return (
        token_grad,
        grad_gate.astype(BF).reshape(1, experts * cut, -1),
        grad_up.astype(BF).reshape(1, experts * cut, -1),
        grad_down.astype(BF).reshape(1, -1, experts * cut),
    )


def solution(mesh):
    fine = Mesh(mesh.devices.reshape(4, 4, 2, 4, 2), ("y", "x", "zh", "zl", "c"))
    tok = ("y", "x", "zh")
    cuts = ("zl", "c")
    hid = ("y", "zl", "c")
    return jax.shard_map(
        shards,
        mesh=fine,
        in_specs=(
            P(tok, cuts),
            P(tok, cuts),
            P(tok, None),
            P(tok, None),
            P(tok, None),
            P(tok, None),
            P(("x", "zh"), None, hid),
            P(("x", "zh"), None, hid),
            P(("x", "zh"), hid, None),
        ),
        out_specs=(
            P(tok, cuts),
            P(("x", "zh"), None, hid),
            P(("x", "zh"), None, hid),
            P(("x", "zh"), hid, None),
        ),
        check_vma=False,
    )
```

time: 396 us -> 237 us (0.60)
  waiting for transfers between devices: 276 us -> 110 us
  matrix products: 45.3 us -> 24.1 us
  starting transfers between devices: 8.05 us -> 29.1 us
  Pallas kernels: 0 us -> 10.7 us
  blocking collectives: 36.6 us -> 26.9 us
    reduce_scatter x1 -> x0, waiting for transfers between devices: 170 us -> none  [shards(): lax.psum_scatter(partial_terms, ('dp', 'cuts'), scatter_dimension=0, tile...]
    ppermute x0 -> x21, waiting for transfers between devices: none -> 33 us  [the longest x3 23.7 us: shards(): up_y = lambda v: lax.ppermute(v.astype(BF), 'y', shift(4, 1)).astype(F32)]
    ppermute x0 -> x21, starting transfers between devices: none -> 29.1 us  [the longest x7 13.7 us: shards(): got = lax.ppermute(parts[flip, :, step], ('zh', 'zl'), zshift(flip, step))]
    all_gather x2 -> x1, waiting for transfers between devices: 106 us -> 77.4 us  [shards(): lax.all_gather(received.reshape(1, slots, 2 * cut), ('y', 'zl', 'c'), axi...]
    dot_general x11 -> x17, matrix products: 45.3 us -> 24.1 us  [the longest x1 6.44 us: shards(): jnp.einsum('hiyb,hys->ibs', token_part, grads_all[..., :units], preferred...]
    pallas_call x0 -> x1, Pallas kernels: none -> 10.7 us  [up_pass(): pl.pallas_call(up_kernel, grid=(blocks,), in_specs=[pl.BlockSpec((1, cuts...]
    all_to_all x2 -> x1, blocking collectives: 36.6 us -> 26.9 us  [shards(): lax.all_to_all(sent.reshape(experts, capacity, 2 * cut), ('x', 'zh'), spl...]
    all_to_all x1 -> x0, starting transfers between devices: 7.93 us -> none  [shards(): lax.all_to_all(own_rows.reshape(experts, capacity, feature_cut), 'expert'...]
  transfers between devices with their start and end apart: 4 -> 22, of which waited for: 3 -> 8; matrix products, arithmetic and copies ran while one was open for 10% -> 12% of each run, Pallas kernels for 0% -> 0%
where the time goes in v1:
time: 237 us; the launch traced here: 235 us
  waiting for transfers between devices  110 us (46%)
  starting transfers between devices  29.1 us (12%)
  blocking collectives  26.9 us (11%)
  matrix products  24.1 us (10%)
  between operations  14.7 us (6%)
  local copies, waits for them, and re-layouts  14.1 us (6%)
  Pallas kernels  10.7 us (5%)
  other arithmetic  5.42 us (2%)
    all_gather x1, waiting for transfers between devices, shards(): lax.all_gather(received.reshape(1, slots, 2 * cut), ('y', 'zl', 'c'), axi...  77.4 us
    all_to_all x1, blocking collectives, shards(): lax.all_to_all(sent.reshape(experts, capacity, 2 * cut), ('x', 'zh'), spl...  26.9 us
    ppermute x3, waiting for transfers between devices, shards(): up_y = lambda v: lax.ppermute(v.astype(BF), 'y', shift(4, 1)).astype(F32)  23.7 us
    ppermute x7, starting transfers between devices, shards(): got = lax.ppermute(parts[flip, :, step], ('zh', 'zl'), zshift(flip, step))  13.7 us
    pallas_call x1, Pallas kernels, up_pass(): pl.pallas_call(up_kernel, grid=(blocks,), in_specs=[pl.BlockSpec((1, cuts...  10.7 us
    dot_general x1, matrix products, shards(): jnp.einsum('hiyb,hys->ibs', token_part, grads_all[..., :units], preferred...  6.44 us
    dot_general x1, matrix products, shards(): jnp.einsum('hpt,hmpu->tmu', hidden, scaled_part, preferred_element_type=F32)  6.42 us
    ppermute x3, starting transfers between devices, shards(): down_y = lambda v: lax.ppermute(v.astype(BF), 'y', shift(4, -1)).astype(F32)  6.22 us
  transfers between devices with their start and end apart: 22, of which 8 were waited for; matrix products, arithmetic and copies ran while one was open for 12% of the time, Pallas kernels for 0%

profile of v1, /device:TPU:2, one launch (start us, length us, event | category | flops | bytes accessed | tf_op | source)
XLA Modules:
  0.0 235.3 jit_solution(7734506893814310939)
XLA Ops:
  7.2 0.8 slice_bitcast_fusion
  8.0 0.7 compare_select_fusion.6
  9.0 1.2 fusion.90
  10.4 0.8 pad_maximum_fusion.2
  11.2 2.0 reshape.59
  13.2 26.9 %all_to_all.5 = bf16[8,36,768]{2,1,0:T(8,128)(2,1)} all-to-all(bf16[8,36,768]{2,1,0:T(8,128)(2,1)} %reshape.59), channel_id=1, replica_groups=mesh['y'=4,'x'=4,'zh'=2,'zl'=4,'c'=2] {'x','zh'}, dimensions={0} | all-to-all | bytes 884736 | tf_op jit(solution)/shard_map/all_to_all | solution.py:103
  40.1 1.9 reshape.60
  42.5 0.6 pad_maximum_fusion
  43.1 1.3 constant_dynamic-slice_fusion.1
  44.3 1.2 constant_dynamic-slice_fusion.2
  45.7 3.9 %collective-permute-done = s32[128,2]{0,1:T(2,128)S(1)} collective-permute-done((s32[128,2]{0,1:T(2,128)S(1)}, s32[128,2]{0,1:T(2,128)S(1)}, u32[]{:S(2)}, u32[]{:S(2)}) %collective-permute-start) | collective-permute-done | bytes 1056 | tf_op jit(solution)/shard_map/ppermute | solution.py:89
  49.8 77.4 %all-gather.2.cloned.1.call-done = bf16[32,288,768]{2,1,0:T(8,128)(2,1)} async-done(((bf16[1,288,768]{2,1,0:T(8,128)(2,1)}), bf16[32,288,768]{2,1,0:T(8,128)(2,1)}) %all-gather.2.cloned.1.call-update) | async-done | bytes 14155792 | tf_op jit(solution)/shard_map/all_gather | solution.py:106
  127.2 1.4 copy-done.2
  128.6 10.7 %shard_map.120 = (bf16[4,288,512]{2,1,0:T(8,128)(2,1)S(1)}, bf16[4,288,256]{2,1,0:T(8,128)(2,1)S(1)}) custom-call(bf16[4,8,288,768]{3,2,1,0:T(8,128)(2,1)} %bitcast.166, bf16[3072,256]{1,0:T(8,128)(2,1)S(1)} %bitcast.142, bf16[3072,256]{1,0:T(8,128)(2,1)S(1)} %bitcast.139, bf16[256,3072]{1,0:T(8,128)(2,1)} %bitcast.172), custom_call_target="tpu_custom_call" | custom-call | flops 5435817984 | bytes 14155776 | tf_op jit(solution)/shard_map/pallas_call | solution.py:51
  139.3 0.7 convolution_convert_fusion
  139.9 0.7 convolution_convert_fusion.2
  140.6 0.3 collective-permute-start.2
  140.9 0.7 convolution_convert_fusion.1
  141.6 0.4 collective-permute-start.3
  141.9 0.4 fusion.61
  142.4 0.3 collective-permute-start.6
  142.7 0.7 convolution_convert_fusion.3
  143.5 0.4 fusion.42
  143.9 0.3 collective-permute-start.1
  144.3 0.2 convert_element_type.115
  144.5 0.4 fusion.15
  144.9 1.4 collective-permute-start.8
  146.3 0.2 convert_element_type.117
  146.6 0.4 fusion.20
  147.0 1.3 collective-permute-start.4
  148.2 0.4 fusion.12
  148.7 2.3 collective-permute-start.9
  151.2 0.4 fusion.19
  151.6 0.7 collective-permute-start.7
  152.4 15.6 %collective-permute-done.4 = bf16[288,768]{1,0:T(8,128)(2,1)S(1)} collective-permute-done((bf16[288,768]{1,0:T(8,128)(2,1)S(1)}, bf16[288,768]{1,0:T(8,128)(2,1)S(1)}, u32[]{:S(2)}, u32[]{:S(2)}) %collective-permute-start.4) | collective-permute-done | bytes 442400 | tf_op jit(solution)/shard_map/ppermute | solution.py:139
  168.2 0.2 collective-permute-start.5
  168.6 3.2 %collective-permute-start.10 = (bf16[288,768]{1,0:T(8,128)(2,1)S(1)}, bf16[288,768]{1,0:T(8,128)(2,1)S(1)}, u32[]{:S(2)}, u32[]{:S(2)}) collective-permute-start(bf16[288,768]{1,0:T(8,128)(2,1)S(1)} %fusion.14), channel_id=1, source_target_pairs={{0,192},{64,0},{128,64},{192,128},{1,193},{65,1},{129,65},{193,129... | collective-permute-start | bytes 1327112 | tf_op jit(solution)/shard_map/ppermute | solution.py:140
  171.8 0.4 fusion.68
  172.2 0.4 fusion.65
  172.7 0.2 convert_element_type.113
  172.9 8.1 %collective-permute-done.5 = bf16[288,768]{1,0:T(8,128)(2,1)S(1)} collective-permute-done((bf16[288,768]{1,0:T(8,128)(2,1)S(1)}, bf16[288,768]{1,0:T(8,128)(2,1)S(1)}, u32[]{:S(2)}, u32[]{:S(2)}) %collective-permute-start.5) | collective-permute-done | bytes 442400 | tf_op jit(solution)/shard_map/ppermute | solution.py:139
  181.0 0.5 fusion.18
  181.6 1.5 collective-permute-start.11
  183.1 1.2 collective-permute-start.12
  184.3 2.1 collective-permute-start.13
  186.4 3.5 %bitcast_convert_fusion.1 = bf16[8,384,256]{2,1,0:T(8,128)(2,1)} fusion(bf16[4,8,288,768]{3,2,1,0:T(8,128)(2,1)S(1)} %bitcast.171, bf16[4,288,512]{2,1,0:T(8,128)(2,1)S(1)} %get-tuple-element.6), kind=kOutput, calls=%fused_computation.8 | convolution fusion | flops 1812725760 | bytes 9240576 | tf_op jit(solution)/shard_map/hiyb,hys->ibs/dot_general | solution.py:188
  189.9 2.7 %collective-permute-done.12 = bf16[72,1536]{1,0:T(8,128)(2,1)S(1)} collective-permute-done((bf16[72,1536]{1,0:T(8,128)(2,1)S(1)}, bf16[72,1536]{1,0:T(8,128)(2,1)S(1)}, u32[]{:S(2)}, u32[]{:S(2)}) %collective-permute-start.12) | collective-permute-done | bytes 221216 | tf_op jit(solution)/shard_map/ppermute | solution.py:159
  192.6 1.7 collective-permute-done.13
  194.3 0.6 convolution_convert_fusion.4
  195.1 1.1 fusion.130
  196.3 3.3 %collective-permute-start.20 = (bf16[128,384]{1,0:T(8,128)(2,1)S(1)}, bf16[128,384]{1,0:T(8,128)(2,1)S(1)}, u32[]{:S(2)}, u32[]{:S(2)}) collective-permute-start(bf16[128,384]{1,0:T(8,128)(2,1)S(1)} %bitcast.165), channel_id=1, source_target_pairs={{0,14},{2,8},{4,10},{6,12},{8,6},{10,0},{12,2},{14,4},{1,15},{3,9}... | collective-permute-start | bytes 294920 | tf_op jit(solution)/shard_map/ppermute | solution.py:178
  199.6 3.0 %collective-permute-start.14 = (bf16[128,384]{1,0:T(8,128)(2,1)S(1)}, bf16[128,384]{1,0:T(8,128)(2,1)S(1)}, u32[]{:S(2)}, u32[]{:S(2)}) collective-permute-start(bf16[128,384]{1,0:T(8,128)(2,1)S(1)} %bitcast.162), channel_id=1, source_target_pairs={{0,2},{2,4},{4,6},{6,0},{8,10},{10,12},{12,14},{14,8},{1,3},{3,5},... | collective-permute-start | bytes 294920 | tf_op jit(solution)/shard_map/ppermute | solution.py:178
  202.6 6.4 %bitcast_convert_fusion.2 = bf16[8,384,256]{2,1,0:T(8,128)(2,1)} fusion(bf16[4,8,288,768]{3,2,1,0:T(8,128)(2,1)} %bitcast.167, bf16[4,288,512]{2,1,0:T(8,128)(2,1)S(1)} %get-tuple-element.6), kind=kOutput, calls=%fused_computation.9 | convolution fusion | flops 1812725760 | bytes 9240576 | tf_op jit(solution)/shard_map/hiyb,hys->ibs/dot_general | solution.py:185
  209.1 0.7 collective-permute-start.15
  209.8 2.3 collective-permute-start.16
  212.1 1.3 collective-permute-start.17
  213.4 2.9 %collective-permute-start.18 = (bf16[128,384]{1,0:T(8,128)(2,1)S(1)}, bf16[128,384]{1,0:T(8,128)(2,1)S(1)}, u32[]{:S(2)}, u32[]{:S(2)}) collective-permute-start(bf16[128,384]{1,0:T(8,128)(2,1)S(1)} %bitcast.160), channel_id=1, source_target_pairs={{0,10},{2,12},{4,14},{6,8},{8,2},{10,4},{12,6},{14,0},{1,11},{3,13... | collective-permute-start | bytes 294920 | tf_op jit(solution)/shard_map/ppermute | solution.py:178
  216.3 0.2 collective-permute-start.19
  216.6 0.4 copy-done.8
  217.0 6.4 %bitcast_convert_fusion = bf16[256,8,384]{2,0,1:T(8,128)(2,1)} fusion(bf16[4,8,288,768]{3,2,1,0:T(8,128)(2,1)} %bitcast.168, bf16[4,288,256]{2,1,0:T(8,128)(2,1)S(1)} %get-tuple-element.7), kind=kOutput, calls=%fused_computation.7 | convolution fusion | flops 1812725760 | bytes 9240576 | tf_op jit(solution)/shard_map/hpt,hmpu->tmu/dot_general | solution.py:191
  223.4 1.7 copy.57
  225.1 1.7 copy.58
  226.9 0.9 collective-permute-done.19
  227.8 0.7 fusion.100
  (71 shorter events, 2.3 us)
Async XLA Ops:
  7.2 120.0 %all-gather.2.cloned.1.call-start = ((), (), s32[]{:S(2)}) async-start(), calls=%async_computation.1 | async-start | bytes 14598144 | tf_op jit(solution)/shard_map/all_gather | solution.py:106
  11.2 30.8 %copy-start.10 = (s32[128,2]{0,1:T(2,128)S(1)}, s32[128,2]{0,1:T(2,128)}, u32[]{:S(2)}) copy-start(s32[128,2]{0,1:T(2,128)} %param.12) | copy-start | bytes 3076
  11.2 31.1 %copy-start = (bf16[1,3072,256]{2,1,0:T(8,128)(2,1)S(1)}, bf16[1,3072,256]{2,1,0:T(8,128)(2,1)}, u32[]{:S(2)}) copy-start(bf16[1,3072,256]{2,1,0:T(8,128)(2,1)} %param.16) | copy-start | bytes 4718596
  11.2 31.1 %copy-start.1 = (bf16[1,3072,256]{2,1,0:T(8,128)(2,1)S(1)}, bf16[1,3072,256]{2,1,0:T(8,128)(2,1)}, u32[]{:S(2)}) copy-start(bf16[1,3072,256]{2,1,0:T(8,128)(2,1)} %param.15) | copy-start | bytes 4718596
  42.1 7.6 %collective-permute-start = (s32[128,2]{0,1:T(2,128)S(1)}, s32[128,2]{0,1:T(2,128)S(1)}, u32[]{:S(2)}, u32[]{:S(2)}) collective-permute-start(s32[128,2]{0,1:T(2,128)S(1)} %compare_select_fusion.5), channel_id=1, source_target_pairs={{0,8},{8,0},{1,9},{9,1},{2,10},{10,2},{3,11},{11,3},{4,12},{12,4},... | collective-permute-start | bytes 3080 | tf_op jit(solution)/shard_map/ppermute | solution.py:89
  127.2 1.4 copy-start.2
  128.6 10.7 %copy-start.3 = (bf16[4,1,384,512]{3,2,1,0:T(8,128)(2,1)S(1)}, bf16[4,1,384,512]{3,2,1,0:T(8,128)(2,1)}, u32[]{:S(2)}) copy-start(bf16[4,1,384,512]{3,2,1,0:T(8,128)(2,1)} %constant_dynamic-slice_fusion.1) | copy-start | bytes 4718596
  140.6 1.4 copy-start.5
  140.6 3.7 %collective-permute-start.2 = (bf16[288,1536]{1,0:T(8,128)(2,1)S(1)}, bf16[288,1536]{1,0:T(8,128)(2,1)S(1)}, u32[]{:S(2)}, u32[]{:S(2)}) collective-permute-start(bf16[288,1536]{1,0:T(8,128)(2,1)S(1)} %convolution_convert_fusion.2), channel_id=1, source_target_pairs={{0,1},{1,0},{2,3},{3,2},{4,5},{5,4},{6,7},{7,6},{8,9},{9,8},{10,11... | collective-permute-start | bytes 2654216 | tf_op jit(solution)/shard_map/ppermute | solution.py:133
  141.6 4.7 %collective-permute-start.3 = (bf16[288,1536]{1,0:T(8,128)(2,1)S(1)}, bf16[288,1536]{1,0:T(8,128)(2,1)S(1)}, u32[]{:S(2)}, u32[]{:S(2)}) collective-permute-start(bf16[288,1536]{1,0:T(8,128)(2,1)S(1)} %convolution_convert_fusion.1), channel_id=1, source_target_pairs={{0,1},{1,0},{2,3},{3,2},{4,5},{5,4},{6,7},{7,6},{8,9},{9,8},{10,11... | collective-permute-start | bytes 2654216 | tf_op jit(solution)/shard_map/ppermute | solution.py:133
  142.4 1.1 copy-start.4
  142.4 8.6 %collective-permute-start.6 = (bf16[288,1536]{1,0:T(8,128)(2,1)S(1)}, bf16[288,1536]{1,0:T(8,128)(2,1)S(1)}, u32[]{:S(2)}, u32[]{:S(2)}) collective-permute-start(bf16[288,1536]{1,0:T(8,128)(2,1)S(1)} %convolution_convert_fusion), channel_id=1, source_target_pairs={{0,1},{1,0},{2,3},{3,2},{4,5},{5,4},{6,7},{7,6},{8,9},{9,8},{10,11... | collective-permute-start | bytes 2654216 | tf_op jit(solution)/shard_map/ppermute | solution.py:133
  143.9 28.7 %collective-permute-start.1 = (bf16[288,1536]{1,0:T(8,128)(2,1)S(1)}, bf16[288,1536]{1,0:T(8,128)(2,1)S(1)}, u32[]{:S(2)}, u32[]{:S(2)}) collective-permute-start(bf16[288,1536]{1,0:T(8,128)(2,1)S(1)} %convolution_convert_fusion.3), channel_id=1, source_target_pairs={{0,1},{1,0},{2,3},{3,2},{4,5},{5,4},{6,7},{7,6},{8,9},{9,8},{10,11... | collective-permute-start | bytes 2654216 | tf_op jit(solution)/shard_map/ppermute | solution.py:133
  144.9 28.0 %collective-permute-start.8 = (bf16[288,768]{1,0:T(8,128)(2,1)S(1)}, bf16[288,768]{1,0:T(8,128)(2,1)S(1)}, u32[]{:S(2)}, u32[]{:S(2)}) collective-permute-start(bf16[288,768]{1,0:T(8,128)(2,1)S(1)} %fusion.15), channel_id=1, source_target_pairs={{0,64},{64,128},{128,192},{192,0},{1,65},{65,129},{129,193},{193,1... | collective-permute-start | bytes 1327112 | tf_op jit(solution)/shard_map/ppermute | solution.py:139
  146.5 39.8 %slice-start = ((s8[14155776]{0:T(1024)(128)(4,1)}), s8[4194304]{0:T(1024)(128)(4,1)S(1)}, s32[]{:S(2)}) async-start(s8[14155776]{0:T(1024)(128)(4,1)} %bitcast.169), calls=%async_computation.2 | async-start | bytes 8388608
  147.0 21.0 %collective-permute-start.4 = (bf16[288,768]{1,0:T(8,128)(2,1)S(1)}, bf16[288,768]{1,0:T(8,128)(2,1)S(1)}, u32[]{:S(2)}, u32[]{:S(2)}) collective-permute-start(bf16[288,768]{1,0:T(8,128)(2,1)S(1)} %fusion.20), channel_id=1, source_target_pairs={{0,64},{64,128},{128,192},{192,0},{1,65},{65,129},{129,193},{193,1... | collective-permute-start | bytes 1327112 | tf_op jit(solution)/shard_map/ppermute | solution.py:139
  148.7 37.7 %slice-start.1 = ((s8[14155776]{0:T(1024)(128)(4,1)}), s8[4194304]{0:T(1024)(128)(4,1)S(1)}, s32[]{:S(2)}) async-start(s8[14155776]{0:T(1024)(128)(4,1)} %bitcast.169), calls=%async_computation.3 | async-start | bytes 8388608
  148.7 19.7 %collective-permute-start.9 = (bf16[288,768]{1,0:T(8,128)(2,1)S(1)}, bf16[288,768]{1,0:T(8,128)(2,1)S(1)}, u32[]{:S(2)}, u32[]{:S(2)}) collective-permute-start(bf16[288,768]{1,0:T(8,128)(2,1)S(1)} %fusion.12), channel_id=1, source_target_pairs={{0,192},{64,0},{128,64},{192,128},{1,193},{65,1},{129,65},{193,129... | collective-permute-start | bytes 1327112 | tf_op jit(solution)/shard_map/ppermute | solution.py:140
  151.6 21.3 %collective-permute-start.7 = (bf16[288,768]{1,0:T(8,128)(2,1)S(1)}, bf16[288,768]{1,0:T(8,128)(2,1)S(1)}, u32[]{:S(2)}, u32[]{:S(2)}) collective-permute-start(bf16[288,768]{1,0:T(8,128)(2,1)S(1)} %fusion.19), channel_id=1, source_target_pairs={{0,192},{64,0},{128,64},{192,128},{1,193},{65,1},{129,65},{193,129... | collective-permute-start | bytes 1327112 | tf_op jit(solution)/shard_map/ppermute | solution.py:140
  168.2 18.2 %slice-start.2 = ((s8[14155776]{0:T(1024)(128)(4,1)}), s8[4194304]{0:T(1024)(128)(4,1)S(1)}, s32[]{:S(2)}) async-start(s8[14155776]{0:T(1024)(128)(4,1)} %bitcast.169), calls=%async_computation.4 | async-start | bytes 8388608
  168.2 12.8 %collective-permute-start.5 = (bf16[288,768]{1,0:T(8,128)(2,1)S(1)}, bf16[288,768]{1,0:T(8,128)(2,1)S(1)}, u32[]{:S(2)}, u32[]{:S(2)}) collective-permute-start(bf16[288,768]{1,0:T(8,128)(2,1)S(1)} %fusion.22), channel_id=1, source_target_pairs={{0,64},{64,128},{128,192},{192,0},{1,65},{65,129},{129,193},{193,1... | collective-permute-start | bytes 1327112 | tf_op jit(solution)/shard_map/ppermute | solution.py:139
  168.6 12.4 %collective-permute-start.10 = (bf16[288,768]{1,0:T(8,128)(2,1)S(1)}, bf16[288,768]{1,0:T(8,128)(2,1)S(1)}, u32[]{:S(2)}, u32[]{:S(2)}) collective-permute-start(bf16[288,768]{1,0:T(8,128)(2,1)S(1)} %fusion.14), channel_id=1, source_target_pairs={{0,192},{64,0},{128,64},{192,128},{1,193},{65,1},{129,65},{193,129... | collective-permute-start | bytes 1327112 | tf_op jit(solution)/shard_map/ppermute | solution.py:140
  172.9 13.5 %slice-start.3 = ((s8[14155776]{0:T(1024)(128)(4,1)}), s8[1572864]{0:T(1024)(128)(4,1)S(1)}, s32[]{:S(2)}) async-start(s8[14155776]{0:T(1024)(128)(4,1)} %bitcast.169), calls=%async_computation.5 | async-start | bytes 3145728
  181.6 8.3 %collective-permute-start.11 = (bf16[72,1536]{1,0:T(8,128)(2,1)S(1)}, bf16[72,1536]{1,0:T(8,128)(2,1)S(1)}, u32[]{:S(2)}, u32[]{:S(2)}) collective-permute-start(bf16[72,1536]{1,0:T(8,128)(2,1)S(1)} %get-tuple-element.27), channel_id=1, source_target_pairs={{0,16},{16,32},{32,48},{48,0},{1,17},{17,33},{33,49},{49,1},{2,18}... | collective-permute-start | bytes 663560 | tf_op jit(solution)/shard_map/ppermute | solution.py:159
  183.1 9.5 %collective-permute-start.12 = (bf16[72,1536]{1,0:T(8,128)(2,1)S(1)}, bf16[72,1536]{1,0:T(8,128)(2,1)S(1)}, u32[]{:S(2)}, u32[]{:S(2)}) collective-permute-start(bf16[72,1536]{1,0:T(8,128)(2,1)S(1)} %get-tuple-element.28), channel_id=1, source_target_pairs={{0,32},{16,48},{32,0},{48,16},{1,33},{17,49},{33,1},{49,17},{2,34}... | collective-permute-start | bytes 663560 | tf_op jit(solution)/shard_map/ppermute | solution.py:159
  184.3 10.0 %collective-permute-start.13 = (bf16[72,1536]{1,0:T(8,128)(2,1)S(1)}, bf16[72,1536]{1,0:T(8,128)(2,1)S(1)}, u32[]{:S(2)}, u32[]{:S(2)}) collective-permute-start(bf16[72,1536]{1,0:T(8,128)(2,1)S(1)} %get-tuple-element.29), channel_id=1, source_target_pairs={{0,48},{16,0},{32,16},{48,32},{1,49},{17,1},{33,17},{49,33},{2,50}... | collective-permute-start | bytes 663560 | tf_op jit(solution)/shard_map/ppermute | solution.py:159
  196.3 17.1 %collective-permute-start.20 = (bf16[128,384]{1,0:T(8,128)(2,1)S(1)}, bf16[128,384]{1,0:T(8,128)(2,1)S(1)}, u32[]{:S(2)}, u32[]{:S(2)}) collective-permute-start(bf16[128,384]{1,0:T(8,128)(2,1)S(1)} %bitcast.165), channel_id=1, source_target_pairs={{0,14},{2,8},{4,10},{6,12},{8,6},{10,0},{12,2},{14,4},{1,15},{3,9}... | collective-permute-start | bytes 294920 | tf_op jit(solution)/shard_map/ppermute | solution.py:178
  199.6 16.8 %collective-permute-start.14 = (bf16[128,384]{1,0:T(8,128)(2,1)S(1)}, bf16[128,384]{1,0:T(8,128)(2,1)S(1)}, u32[]{:S(2)}, u32[]{:S(2)}) collective-permute-start(bf16[128,384]{1,0:T(8,128)(2,1)S(1)} %bitcast.162), channel_id=1, source_target_pairs={{0,2},{2,4},{4,6},{6,0},{8,10},{10,12},{12,14},{14,8},{1,3},{3,5},... | collective-permute-start | bytes 294920 | tf_op jit(solution)/shard_map/ppermute | solution.py:178
  209.1 17.8 %collective-permute-start.15 = (bf16[128,384]{1,0:T(8,128)(2,1)S(1)}, bf16[128,384]{1,0:T(8,128)(2,1)S(1)}, u32[]{:S(2)}, u32[]{:S(2)}) collective-permute-start(bf16[128,384]{1,0:T(8,128)(2,1)S(1)} %bitcast.164), channel_id=1, source_target_pairs={{0,4},{2,6},{4,0},{6,2},{8,12},{10,14},{12,8},{14,10},{1,5},{3,7},... | collective-permute-start | bytes 294920 | tf_op jit(solution)/shard_map/ppermute | solution.py:178
  209.8 17.0 %collective-permute-start.16 = (bf16[128,384]{1,0:T(8,128)(2,1)S(1)}, bf16[128,384]{1,0:T(8,128)(2,1)S(1)}, u32[]{:S(2)}, u32[]{:S(2)}) collective-permute-start(bf16[128,384]{1,0:T(8,128)(2,1)S(1)} %bitcast.163), channel_id=1, source_target_pairs={{0,6},{2,0},{4,2},{6,4},{8,14},{10,8},{12,10},{14,12},{1,7},{3,1},... | collective-permute-start | bytes 294920 | tf_op jit(solution)/shard_map/ppermute | solution.py:178
  212.1 14.8 %collective-permute-start.17 = (bf16[128,384]{1,0:T(8,128)(2,1)S(1)}, bf16[128,384]{1,0:T(8,128)(2,1)S(1)}, u32[]{:S(2)}, u32[]{:S(2)}) collective-permute-start(bf16[128,384]{1,0:T(8,128)(2,1)S(1)} %bitcast.161), channel_id=1, source_target_pairs={{0,8},{2,10},{4,12},{6,14},{8,0},{10,2},{12,4},{14,6},{1,9},{3,11}... | collective-permute-start | bytes 294920 | tf_op jit(solution)/shard_map/ppermute | solution.py:178
  213.4 3.2 %copy-start.6 = (bf16[128,384]{1,0:T(8,128)(2,1)}, bf16[128,384]{1,0:T(8,128)(2,1)S(1)}, u32[]{:S(2)}) copy-start(bf16[128,384]{1,0:T(8,128)(2,1)S(1)} %collective-permute-done.20) | copy-start | bytes 294916
  213.4 13.5 %collective-permute-start.18 = (bf16[128,384]{1,0:T(8,128)(2,1)S(1)}, bf16[128,384]{1,0:T(8,128)(2,1)S(1)}, u32[]{:S(2)}, u32[]{:S(2)}) collective-permute-start(bf16[128,384]{1,0:T(8,128)(2,1)S(1)} %bitcast.160), channel_id=1, source_target_pairs={{0,10},{2,12},{4,14},{6,8},{8,2},{10,4},{12,6},{14,0},{1,11},{3,13... | collective-permute-start | bytes 294920 | tf_op jit(solution)/shard_map/ppermute | solution.py:178
  216.3 0.6 copy-start.8
  216.3 11.4 %collective-permute-start.19 = (bf16[128,384]{1,0:T(8,128)(2,1)S(1)}, bf16[128,384]{1,0:T(8,128)(2,1)S(1)}, u32[]{:S(2)}, u32[]{:S(2)}) collective-permute-start(bf16[128,384]{1,0:T(8,128)(2,1)S(1)} %bitcast.159), channel_id=1, source_target_pairs={{0,12},{2,14},{4,8},{6,10},{8,4},{10,6},{12,0},{14,2},{1,13},{3,15... | collective-permute-start | bytes 294920 | tf_op jit(solution)/shard_map/ppermute | solution.py:178
  225.1 2.6 %copy-start.7 = (bf16[128,384]{1,0:T(8,128)(2,1)S(1)}, bf16[128,384]{1,0:T(8,128)(2,1)}, u32[]{:S(2)}) copy-start(bf16[128,384]{1,0:T(8,128)(2,1)} %copy-done.6) | copy-start | bytes 294916
  225.1 2.6 %copy-start.9 = (bf16[128,384]{1,0:T(8,128)(2,1)S(1)}, bf16[128,384]{1,0:T(8,128)(2,1)}, u32[]{:S(2)}) copy-start(bf16[128,384]{1,0:T(8,128)(2,1)} %copy-done.8) | copy-start | bytes 294916
Sparse Core Ops, SparseCore 0:
  42.2 84.9 all-gather.1
